TPU v7x, 256 devices: a whole 4x4x8 slice. The times are simulated.
256 devices in a mesh: wa: 128 (over z, x_hi, y, core), gy: 2 (over x_lo).
Axes of the slice: x: 4 (x_hi: 2, x_lo: 2; x = x_hi * 2 + x_lo), y: 4, z: 8, core: 2. Of those that a mesh axis runs over, the one named last changes fastest.
Arguments:
- input_moments: float32 [120, 1024, 256], P(None, 'wa', 'gy'), may hold values from -6 to 6
- solid_cell_mask: int32 [1024, 256], P('wa', 'gy'), may hold values 0 or 1
- collision_coefficients: float32 [120, 120], replicated, may hold values from -0.5 to 0.5
- relaxation_rates: float32 [120], replicated, may hold values from 0.1 to 1
Outputs:
- final_state: float32 [120, 1024, 256], P(None, 'wa', 'gy')
All inputs are finite; a program needn't handle non-finite values. No bound on the sum of `solid_cell_mask` on one device may be relied on, other than what follows from the above.
Results may differ from a plain program's by a relative error of at most 0.0003.
Values sent between devices are 32-bit elements; how exact they have to be, the bound alone decides.
A program may use at most 64 MiB of HBM per device.

v0:
```python
import functools
import math

import jax
import jax.numpy as jnp
import ml_dtypes
import numpy as np
from jax import lax
from jax.experimental import pallas as pl
from jax.experimental.pallas import tpu as pltpu
from jax.sharding import PartitionSpec as P

DEG = 7
AXIAL_STEP = 0.2
CROSS_STEP = 0.2
COLLIDE_STEP = 0.5
NX = 1024
LINES = 128
OWN = 8
LANES = 128
MOMENTS = 120
MASK_LANE = 120
HALF = 72
BLOCKS = HALF // 8
ROOT_HALF = math.sqrt(0.5)

F32 = jnp.float32
BF16 = jnp.bfloat16
MESH = pl.DeviceIdType.MESH


def moment_table():
    entries = []
    for degree in range(DEG + 1):
        for k1 in range(degree, -1, -1):
            for k2 in range(degree - k1, -1, -1):
                entries.append((k1, k2, degree - k1 - k2))
    return entries


def hermite(order, point):
    previous, current = 0.0, 1.0
    for level in range(order):
        previous, current = current, point * current - level * previous
    return current


def hermite_roots(order):
    roots, step = [], 1.0 / 128
    low = -(2.0 * math.sqrt(order) + 1.0) - step / 3
    while len(roots) < order:
        high = low + step
        if (hermite(order, low) > 0) != (hermite(order, high) > 0):
            a, b = low, high
            for _ in range(80):
                middle = 0.5 * (a + b)
                if (hermite(order, middle) > 0) == (hermite(order, a) > 0):
                    a = middle
                else:
                    b = middle
            roots.append(0.5 * (a + b))
        low = high
    return roots


def coupling(entries, lookup, direction):
    matrix = np.zeros((LANES, LANES))
    for position, moment in enumerate(entries):
        raised = list(moment)
        raised[direction] += 1
        partner = lookup.get(tuple(raised))
        if partner is not None:
            matrix[position, partner] = matrix[partner, position] = math.sqrt(raised[direction])
    return matrix


def axial_modes(lookup):
    values = np.zeros(LANES)
    vectors = np.zeros((LANES, LANES))
    column = 0
    for k2 in range(DEG + 1):
        for k3 in range(DEG + 1 - k2):
            size = DEG + 1 - k2 - k3
            for root in hermite_roots(size):
                entry = [hermite(k, root) / math.sqrt(math.factorial(k)) for k in range(size)]
                norm = math.sqrt(sum(v * v for v in entry))
                for k in range(size):
                    vectors[lookup[k, k2, k3], column] = entry[k] / norm
                values[column] = root
                column += 1
    return values, vectors


def parts(table):
    high = table.astype(np.float32).astype(ml_dtypes.bfloat16)
    low = (table - high.astype(np.float64)).astype(np.float32).astype(ml_dtypes.bfloat16)
    return high, low


def right_factor(table):
    high, low = parts(table)
    return np.block([[high, low], [high, np.zeros_like(low)]])


@functools.cache
def tables():
    entries = moment_table()
    lookup = {moment: position for position, moment in enumerate(entries)}
    values, modes = axial_modes(lookup)
    a2 = coupling(entries, lookup, 1)
    speed = hermite_roots(DEG + 1)[-1]
    eye = np.eye(LANES)

    high, low = parts(modes.T)
    to_modes = np.concatenate([high, high, low], axis=1)

    k1 = np.arange(HALF)
    used = k1 <= 64
    weight = np.where(used, np.where((k1 == 0) | (k1 == 64), 1.0, 2.0), 0.0) / NX
    line = np.arange(LINES)
    forward, inverse = [], []
    for own in range(OWN):
        phase = (((OWN * line + own)[:, None] * k1[None, :]) % NX) * (2 * math.pi / NX)
        cosine, sine = np.cos(phase) * used, np.sin(phase) * used
        forward.append(np.concatenate(parts(np.concatenate([cosine.T, -sine.T], axis=0)), axis=1))
        inverse.append(np.concatenate(parts(np.concatenate([cosine * weight, -sine * weight], axis=1)), axis=0))
    forward, inverse = np.stack(forward), np.stack(inverse)

    wave = k1[None, :] + 128 * np.arange(8)[:, None]
    wave = np.where(wave < NX // 2, wave, wave - NX) * (AXIAL_STEP * 2 * math.pi / NX)
    angle = (wave[:, :, None] * values) * used[None, :, None]
    series = np.stack([1 - angle**2 / 2 + angle**4 / 24, -(angle - angle**3 / 6)])
    series = series.astype(np.float32)

    here = modes.T * (1 - CROSS_STEP * speed)
    upper = modes.T @ (0.5 * CROSS_STEP * (speed * eye - a2))
    lower = modes.T @ (0.5 * CROSS_STEP * (speed * eye + a2))
    cross = np.stack(
        [np.concatenate([right_factor(m) for m in order]) for order in ((here, upper, lower), (here, lower, upper))]
    )

    degrees = np.array([sum(moment) for moment in entries] + [0] * (LANES - MOMENTS))
    band = (np.abs(degrees[:, None] - degrees[None, :]) <= 1) & (degrees[:, None] >= 2) & (degrees[None, :] >= 2)
    first, second = np.zeros((LANES, LANES)), np.zeros((LANES, LANES))
    rows = np.zeros((8, LANES), np.float32)
    units = [lookup[1, 0, 0], lookup[0, 1, 0], lookup[0, 0, 1]]
    for position, moment in enumerate(entries):
        if sum(moment) == 2:
            d = [direction for direction in range(3) for _ in range(moment[direction])]
            first[units[d[0]], position] = 1.0
            second[units[d[1]], position] = 1.0
            rows[0, position] = COLLIDE_STEP * (ROOT_HALF if d[0] == d[1] else 1.0)
    pick = np.concatenate([first, second], axis=1)
    pick = np.concatenate([pick, pick], axis=0).astype(ml_dtypes.bfloat16)
    rows[1] = COLLIDE_STEP * (degrees >= 2)
    band = (band * COLLIDE_STEP).astype(np.float32)
    modes_right = right_factor(modes)
    return dict(
        to_modes=to_modes, forward=forward, inverse=inverse, series=series, cross=cross, band=band, rows=rows, pick=pick,
        modes_right=modes_right,
    )


def split(a):
    high = a.astype(BF16)
    return high, (a - high.astype(F32)).astype(BF16)


def fold(a):
    return a[:, :LANES] + a[:, LANES:]


def add(a, b):
    return (a[0] + b[0], a[1] + b[1])


def sub(a, b):
    return (a[0] - b[0], a[1] - b[1])


def quarter(a, sign):
    return (-a[1], a[0]) if sign > 0 else (a[1], -a[0])


def fourier4(v, sign):
    s, d = add(v[0], v[2]), sub(v[0], v[2])
    t, e = add(v[1], v[3]), quarter(sub(v[1], v[3]), sign)
    return [add(s, t), add(d, e), sub(s, t), sub(d, e)]


def fourier8(v, sign):
    even, odd = fourier4(v[0::2], sign), fourier4(v[1::2], sign)
    turned = [
        odd[0],
        ((odd[1][0] - sign * odd[1][1]) * ROOT_HALF, (odd[1][1] + sign * odd[1][0]) * ROOT_HALF),
        quarter(odd[2], sign),
        ((-odd[3][0] - sign * odd[3][1]) * ROOT_HALF, (-odd[3][1] + sign * odd[3][0]) * ROOT_HALF),
    ]
    return [add(a, b) for a, b in zip(even, turned)] + [sub(a, b) for a, b in zip(even, turned)]


def device_at(place):
    chip, core = place // 2, place % 2
    x_hi = chip // 32
    turn = chip % 32
    turn = turn + x_hi * (31 - 2 * turn)
    z = turn // 4
    y = turn % 4
    y = y + (z % 2) * (3 - 2 * y)
    return ((z * 2 + x_hi) * 4 + y) * 2 + core


def place_of(device):
    core, y, x_hi, z = device % 2, (device // 2) % 4, (device // 8) % 2, device // 16
    turn = z * 4 + y + (z % 2) * (3 - 2 * y)
    return (x_hi * 32 + turn + x_hi * (31 - 2 * turn)) * 2 + core


def kernel(
    x_ref, mask_ref, c_ref, rate_ref,
    to_modes_h, forward_h, inverse_h, series_h, cross_h, band_h, rows_h, pick_h, modes_h,
    out_ref,
    to_modes, forward, inverse, series, cross, band, rows, pick, modes,
    send1, recv1, send2, recv2, lines, beside, wall, spectrum, square, rate_row, collide,
    table_sem, send_sem, recv_sem, edge_send, edge_recv, near_send, near_recv,
):
    me, slab = lax.axis_index("wa"), lax.axis_index("gy")
    place = place_of(me)
    my_line = place + slab * (LINES - 1 - 2 * place)
    is_edge = place // (LINES - 1)
    next_wa, next_gy = device_at(place + 1 - is_edge), slab + is_edge * (1 - 2 * slab)
    is_first = 1 - (place + LINES - 1) // LINES
    prev_wa, prev_gy = device_at(place - 1 + is_first), slab + is_first * (1 - 2 * slab)

    barrier = pltpu.get_barrier_semaphore()

    @pl.loop(1, LINES)
    def _(step):
        pl.semaphore_signal(barrier, inc=1, device_id=((me + step) % LINES, slab), device_id_type=MESH)

    pl.semaphore_signal(barrier, inc=1, device_id=(me, 1 - slab), device_id_type=MESH)

    loads = [
        pltpu.make_async_copy(src, dst, table_sem.at[i])
        for i, (src, dst) in enumerate(
            [(to_modes_h, to_modes), (forward_h, forward), (series_h, series), (inverse_h, inverse), (cross_h.at[slab], cross.at[0]),
             (cross_h.at[0], cross.at[1]), (band_h, band), (rows_h, rows), (pick_h, pick), (modes_h, modes)]
        )
    ]
    for load in loads:
        load.start()
    loads[0].wait()

    row = lax.broadcasted_iota(jnp.int32, (LANES, LANES), 0)
    lane = lax.broadcasted_iota(jnp.int32, (LANES, LANES), 1)

    @pl.loop(0, OWN)
    def _(own):
        cells = x_ref[pl.ds(own, MOMENTS, stride=OWN), :]
        cells = jnp.concatenate([cells, jnp.zeros((LANES - MOMENTS, LANES), F32)], axis=0)
        high, low = split(cells)
        turned = jnp.dot(to_modes[...], jnp.concatenate([high, low, high], axis=0), preferred_element_type=F32)
        flags = mask_ref[pl.ds(own, 1), :].astype(F32)
        turned = jnp.where(row == MASK_LANE, flags, turned)
        send1[pl.ds(own, LINES, stride=OWN), :] = turned.T

    pl.semaphore_wait(barrier, LINES)

    @pl.loop(1, LINES)
    def _(step):
        target = (me + step) % LINES
        target_place = place_of(target)
        target_line = target_place + slab * (LINES - 1 - 2 * target_place)
        pltpu.make_async_remote_copy(
            src_ref=send1.at[pl.ds(pl.multiple_of(target_line * OWN, OWN), OWN), :],
            dst_ref=recv1.at[pl.ds(pl.multiple_of(me * OWN, OWN), OWN), :],
            send_sem=send_sem.at[0],
            recv_sem=recv_sem.at[0],
            device_id=(target, slab),
            device_id_type=MESH,
        ).start()

    recv1[pl.ds(pl.multiple_of(me * OWN, OWN), OWN), :] = send1[pl.ds(pl.multiple_of(my_line * OWN, OWN), OWN), :]

    for load in loads[1:]:
        load.wait()
    square[...] = jnp.zeros_like(square)
    square[:MOMENTS, :MOMENTS] = c_ref[...]
    rate_row[...] = jnp.zeros_like(rate_row)
    rate_row[:, :MOMENTS] = rate_ref[...]
    rates = rate_row[...] * rows[1:2, :]
    linear = (square[...] * band[...]).T + jnp.where(row == lane, 1.0 - rates, 0.0)
    high, low = split(linear)
    collide[...] = jnp.concatenate(
        [jnp.concatenate([high, low], axis=1), jnp.concatenate([high, jnp.zeros_like(low)], axis=1)], axis=0
    )
    drive = rate_row[...] * rows[0:1, :]

    def finish(here, after, before, factor, keep):
        operand = jnp.concatenate([*split(here), *split(after), *split(before)], axis=1)
        f = fold(jnp.dot(operand, factor, preferred_element_type=F32)) * keep
        operand = jnp.concatenate(split(f), axis=1)
        mixed = fold(jnp.dot(operand, collide[...], preferred_element_type=F32))
        chosen = jnp.dot(operand, pick[...], preferred_element_type=F32)
        return mixed + drive * (chosen[:, :LANES] * chosen[:, LANES:])

    def to_spectrum(own, cells):
        high, low = split(cells)
        table = forward[own]
        operand = jnp.concatenate([table[:, :LANES], table], axis=1)
        spectrum[own] = jnp.dot(operand, jnp.concatenate([high, low, high], axis=0), preferred_element_type=F32)

    def advance():
        @pl.loop(0, BLOCKS)
        def _(block):
            at = pl.multiple_of(block * 8, 8)
            re, im = pl.ds(at, 8), pl.ds(pl.multiple_of(HALF + at, 8), 8)
            f = fourier8([(spectrum[own, re, :], spectrum[own, im, :]) for own in range(OWN)], -1)
            h = []
            for k, (fr, fi) in enumerate(f):
                pr, pi = series[0, k, re, :], series[1, k, re, :]
                h.append((pr * fr - pi * fi, pr * fi + pi * fr))
            for own, (ur, ui) in enumerate(fourier8(h, 1)):
                spectrum[own, re, :] = ur
                spectrum[own, im, :] = ui

    def from_spectrum(own):
        high, low = split(spectrum[own])
        table = inverse[own]
        main = jnp.dot(table[:LINES], jnp.concatenate([high, low], axis=1), preferred_element_type=F32)
        return fold(main) + jnp.dot(table[LINES:], high, preferred_element_type=F32)

    rest = pl.ds(0, (LINES - 1) * OWN)
    pltpu.make_async_copy(recv1.at[rest, :], recv1.at[rest, :], recv_sem.at[0]).wait()

    @pl.loop(0, OWN)
    def _(own):
        cells = recv1[pl.ds(own, LINES, stride=OWN), :]
        flags = jnp.broadcast_to(cells[:, MASK_LANE : MASK_LANE + 1], (LINES, LANES))
        wall[own] = jnp.where(lane == 0, 1.0, 1.0 - flags)
        to_spectrum(own, cells)

    advance()

    def near(own, which):
        slot = 1 - is_first if which else is_edge
        return pltpu.make_async_remote_copy(
            src_ref=lines.at[own],
            dst_ref=beside.at[slot, own],
            send_sem=near_send.at[which, own],
            recv_sem=near_recv.at[slot, own],
            device_id=(prev_wa, prev_gy) if which else (next_wa, next_gy),
            device_id_type=MESH,
        )

    @pl.loop(0, OWN)
    def _(own):
        lines[own] = from_spectrum(own)
        near(own, 0).start()
        near(own, 1).start()

    inside = 1.0 - is_first.astype(F32)

    @pl.loop(0, OWN)
    def _(own):
        for slot in range(2):
            pltpu.make_async_copy(lines.at[own], beside.at[slot, own], near_recv.at[slot, own]).wait()
        f = finish(lines[own], beside[1, own], beside[0, own] * inside, cross[0], wall[own])
        f = fold(jnp.dot(jnp.concatenate(split(f), axis=1), modes[...], preferred_element_type=F32))
        to_spectrum(own, f)

    advance()

    @pl.loop(0, OWN)
    def _(own):
        send2[pl.ds(own, LINES, stride=OWN), :] = from_spectrum(own)

    my_tile = pl.ds(pl.multiple_of((my_line + 1) * OWN, OWN), OWN)

    @pl.loop(1, LINES)
    def _(step):
        target = (me + step) % LINES
        pltpu.make_async_remote_copy(
            src_ref=send2.at[pl.ds(pl.multiple_of(target * OWN, OWN), OWN), :],
            dst_ref=recv2.at[my_tile, :],
            send_sem=send_sem.at[1],
            recv_sem=recv_sem.at[1 + is_edge],
            device_id=(target, slab),
            device_id_type=MESH,
        ).start()

    recv2[my_tile, :] = send2[pl.ds(pl.multiple_of(me * OWN, OWN), OWN), :]
    outside = pl.ds(pl.multiple_of(slab * (LINES + 1) * OWN, OWN), OWN)
    recv2[outside, :] = jnp.zeros((OWN, LANES), F32)

    edge_tile = pl.ds(pl.multiple_of((LINES - slab * (LINES - 1)) * OWN, OWN), OWN)

    @pl.when(is_edge == 0)
    def _():
        one = pl.ds(0, OWN)
        pltpu.make_async_copy(recv2.at[one, :], recv2.at[one, :], recv_sem.at[2]).wait()

    beyond = pltpu.make_async_remote_copy(
        src_ref=recv2.at[edge_tile, :],
        dst_ref=recv2.at[outside, :],
        send_sem=edge_send,
        recv_sem=edge_recv,
        device_id=(me, 1 - slab),
        device_id_type=MESH,
    )
    beyond.start()

    @pl.when(is_edge == 1)
    def _():
        pltpu.make_async_copy(recv2.at[rest, :], recv2.at[rest, :], recv_sem.at[1]).wait()

    @pl.when(is_edge == 0)
    def _():
        less = pl.ds(0, (LINES - 2) * OWN)
        pltpu.make_async_copy(recv2.at[less, :], recv2.at[less, :], recv_sem.at[1]).wait()

    beyond.wait()

    @pl.loop(0, OWN)
    def _(own):
        flags = send1[pl.ds(own, LINES, stride=OWN), :][:, MASK_LANE : MASK_LANE + 1]
        keep = jnp.where(lane == 0, 1.0, 1.0 - jnp.broadcast_to(flags, (LINES, LANES)))
        f = finish(
            recv2[pl.ds(OWN + own, LINES, stride=OWN), :],
            recv2[pl.ds(2 * OWN + own, LINES, stride=OWN), :],
            recv2[pl.ds(own, LINES, stride=OWN), :],
            cross[1],
            keep,
        )
        out_ref[pl.ds(own, MOMENTS, stride=OWN), :] = f.T[:MOMENTS]

    @pl.loop(0, OWN)
    def _(own):
        near(own, 0).wait_send()
        near(own, 1).wait_send()

    pltpu.make_async_copy(send1.at[rest, :], send1.at[rest, :], send_sem.at[0]).wait()
    pltpu.make_async_copy(send2.at[rest, :], send2.at[rest, :], send_sem.at[1]).wait()


def local(moments, mask, coefficients, rates):
    t = tables()
    names = ["to_modes", "forward", "inverse", "series", "cross", "band", "rows", "pick", "modes_right"]
    constants = [jnp.asarray(t[name]) for name in names]
    in_vmem = pl.BlockSpec(memory_space=pltpu.VMEM)
    anywhere = pl.BlockSpec(memory_space=pl.ANY)
    tile = (NX, LANES)
    line = (OWN, LINES, LANES)
    out = pl.pallas_call(
        kernel,
        out_shape=jax.ShapeDtypeStruct((MOMENTS * OWN, LINES), F32),
        in_specs=[in_vmem] * 4 + [anywhere] * len(constants),
        out_specs=in_vmem,
        scratch_shapes=[pltpu.VMEM(c.shape, c.dtype) for c in constants]
        + [pltpu.VMEM(shape, F32) for shape in (tile, tile, tile, (NX + 2 * OWN, LANES), line, (2, *line), line, (OWN, 2 * HALF, LANES), (LANES, LANES), (1, LANES))]
        + [
            pltpu.VMEM((2 * LANES, 2 * LANES), BF16),
            pltpu.SemaphoreType.DMA((10,)),
            pltpu.SemaphoreType.DMA((2,)),
            pltpu.SemaphoreType.DMA((3,)),
            pltpu.SemaphoreType.DMA,
            pltpu.SemaphoreType.DMA,
            pltpu.SemaphoreType.DMA((2, OWN)),
            pltpu.SemaphoreType.DMA((2, OWN)),
        ],
        compiler_params=pltpu.CompilerParams(collective_id=0, has_side_effects=True, vmem_limit_bytes=48 * 1024 * 1024),
        name="duct",
    )(
        moments.reshape(MOMENTS * OWN, LINES),
        mask,
        coefficients,
        rates.reshape(1, MOMENTS),
        *constants,
    )
    return out.reshape(MOMENTS, OWN, LINES)


def solution(mesh):
    in_specs = (P(None, "wa", "gy"), P("wa", "gy"), P(), P())
    return jax.shard_map(local, mesh=mesh, in_specs=in_specs, out_specs=P(None, "wa", "gy"), check_vma=False)
```

profile of v0, /device:TPU:1, one launch (start us, length us, event | category | flops | bytes accessed | tf_op | source)
XLA Modules:
  0.0 75.8 jit_solution(17454141931981455912)
XLA Ops:
  0.0 0.0 copy-start.11
  0.0 0.0 copy-start.12
  0.0 0.7 copy-done.11
  0.7 0.0 copy-done.12
  0.7 0.0 copy-start
  0.7 1.2 %copy-done = bf16[8,256,144]{2,1,0:T(8,128)(2,1)S(1)} copy-done((bf16[8,256,144]{2,1,0:T(8,128)(2,1)S(1)}, bf16[8,256,144]{2,1,0:T(8,128)(2,1)}, u32[]{:S(2)}) %copy-start) | copy-done | bytes 589848
  1.9 0.0 copy-start.1
  1.9 1.1 %copy-done.1 = bf16[2,768,256]{2,1,0:T(8,128)(2,1)S(1)} copy-done((bf16[2,768,256]{2,1,0:T(8,128)(2,1)S(1)}, bf16[2,768,256]{2,1,0:T(8,128)(2,1)}, u32[]{:S(2)}) %copy-start.1) | copy-done | bytes 786456
  3.0 0.0 copy-start.2
  3.1 1.1 %copy-done.2 = f32[2,8,72,128]{3,2,1,0:T(8,128)S(1)} copy-done((f32[2,8,72,128]{3,2,1,0:T(8,128)S(1)}, f32[2,8,72,128]{3,2,1,0:T(8,128)}, u32[]{:S(2)}) %copy-start.2) | copy-done | bytes 589848
  4.1 0.0 copy-start.3
  4.1 1.1 %copy-done.3 = bf16[8,144,256]{2,1,0:T(8,128)(2,1)S(1)} copy-done((bf16[8,144,256]{2,1,0:T(8,128)(2,1)S(1)}, bf16[8,144,256]{2,1,0:T(8,128)(2,1)}, u32[]{:S(2)}) %copy-start.3) | copy-done | bytes 589848
  5.2 0.0 copy-start.4
  5.2 1.0 %copy-done.4 = f32[120,8,128]{2,1,0:T(8,128)S(1)} copy-done((f32[120,8,128]{2,1,0:T(8,128)S(1)}, f32[120,8,128]{2,1,0:T(8,128)}, u32[]{:S(2)}) %copy-start.4) | copy-done | bytes 491544
  6.2 0.0 copy-start.5
  6.2 0.9 %copy-done.5 = bf16[256,256]{1,0:T(8,128)(2,1)S(1)} copy-done((bf16[256,256]{1,0:T(8,128)(2,1)S(1)}, bf16[256,256]{1,0:T(8,128)(2,1)}, u32[]{:S(2)}) %copy-start.5) | copy-done | bytes 131096
  7.1 0.0 copy-start.6
  7.1 0.9 %copy-done.6 = bf16[256,256]{1,0:T(8,128)(2,1)S(1)} copy-done((bf16[256,256]{1,0:T(8,128)(2,1)S(1)}, bf16[256,256]{1,0:T(8,128)(2,1)}, u32[]{:S(2)}) %copy-start.6) | copy-done | bytes 131096
  8.0 0.0 copy-start.7
  8.0 0.9 %copy-done.7 = bf16[128,384]{1,0:T(8,128)(2,1)S(1)} copy-done((bf16[128,384]{1,0:T(8,128)(2,1)S(1)}, bf16[128,384]{1,0:T(8,128)(2,1)}, u32[]{:S(2)}) %copy-start.7) | copy-done | bytes 98328
  8.9 0.0 copy-start.8
  8.9 0.8 %copy-done.8 = f32[128,128]{1,0:T(8,128)S(1)} copy-done((f32[128,128]{1,0:T(8,128)S(1)}, f32[128,128]{1,0:T(8,128)}, u32[]{:S(2)}) %copy-start.8) | copy-done | bytes 65560
  9.8 0.0 copy-start.9
  9.8 0.8 %copy-done.9 = f32[120,120]{1,0:T(8,128)S(1)} copy-done((f32[120,120]{1,0:T(8,128)S(1)}, f32[120,120]{1,0:T(8,128)}, u32[]{:S(2)}) %copy-start.9) | copy-done | bytes 57624
  10.6 0.0 copy-start.10
  10.6 0.7 copy-done.10
  11.3 63.7 %duct.1 = f32[960,128]{1,0:T(8,128)S(1)} custom-call(f32[960,128]{1,0:T(8,128)S(1)} %bitcast.4, s32[8,128]{1,0:T(8,128)S(1)} %copy-done.10, f32[120,120]{1,0:T(8,128)S(1)} %copy-done.9, f32[1,120]{1,0:T(1,128)S(1)} %bitcast.5, bf16[128,384]{1,0:T(8,128)(2,1)S(1)} %copy-done.7, bf16[8,144,256]{2,1,0:T(8,128)(2,1)S(1)} %copy-done.3, ...), custom_call_target="tpu_custom_call" | custom-call | tf_op jit(solution)/shard_map/duct/pallas_call | solution.py:454
  75.0 0.8 %copy.15 = f32[120,8,128]{2,1,0:T(8,128)} copy(f32[120,8,128]{2,1,0:T(8,128)S(1)} %bitcast.3) | data formatting | bytes 983040
Async XLA Ops:
  0.0 0.7 copy-start.11
  0.0 0.7 copy-start.12
  0.7 1.2 %copy-start = (bf16[8,256,144]{2,1,0:T(8,128)(2,1)S(1)}, bf16[8,256,144]{2,1,0:T(8,128)(2,1)}, u32[]{:S(2)}) copy-start(bf16[8,256,144]{2,1,0:T(8,128)(2,1)} %constant.20.clone.inverse_h) | copy-start | bytes 1769476
  1.9 1.1 %copy-start.1 = (bf16[2,768,256]{2,1,0:T(8,128)(2,1)S(1)}, bf16[2,768,256]{2,1,0:T(8,128)(2,1)}, u32[]{:S(2)}) copy-start(bf16[2,768,256]{2,1,0:T(8,128)(2,1)} %constant.22.clone.cross_h) | copy-start | bytes 2359300
  3.0 1.1 %copy-start.2 = (f32[2,8,72,128]{3,2,1,0:T(8,128)S(1)}, f32[2,8,72,128]{3,2,1,0:T(8,128)}, u32[]{:S(2)}) copy-start(f32[2,8,72,128]{3,2,1,0:T(8,128)} %constant.21.clone.series_h) | copy-start | bytes 1769476
  4.1 1.1 %copy-start.3 = (bf16[8,144,256]{2,1,0:T(8,128)(2,1)S(1)}, bf16[8,144,256]{2,1,0:T(8,128)(2,1)}, u32[]{:S(2)}) copy-start(bf16[8,144,256]{2,1,0:T(8,128)(2,1)} %constant.19.clone.forward_h) | copy-start | bytes 1769476
  5.2 1.0 %copy-start.4 = (f32[120,8,128]{2,1,0:T(8,128)S(1)}, f32[120,8,128]{2,1,0:T(8,128)}, u32[]{:S(2)}) copy-start(f32[120,8,128]{2,1,0:T(8,128)} %param.13) | copy-start | bytes 1474564
  6.2 0.9 %copy-start.5 = (bf16[256,256]{1,0:T(8,128)(2,1)S(1)}, bf16[256,256]{1,0:T(8,128)(2,1)}, u32[]{:S(2)}) copy-start(bf16[256,256]{1,0:T(8,128)(2,1)} %constant.26.clone.modes_h) | copy-start | bytes 393220
  7.1 0.9 %copy-start.6 = (bf16[256,256]{1,0:T(8,128)(2,1)S(1)}, bf16[256,256]{1,0:T(8,128)(2,1)}, u32[]{:S(2)}) copy-start(bf16[256,256]{1,0:T(8,128)(2,1)} %constant.25.clone.pick_h) | copy-start | bytes 393220
  8.0 0.9 %copy-start.7 = (bf16[128,384]{1,0:T(8,128)(2,1)S(1)}, bf16[128,384]{1,0:T(8,128)(2,1)}, u32[]{:S(2)}) copy-start(bf16[128,384]{1,0:T(8,128)(2,1)} %constant.18.clone.to_modes_h) | copy-start | bytes 294916
  8.9 0.8 %copy-start.8 = (f32[128,128]{1,0:T(8,128)S(1)}, f32[128,128]{1,0:T(8,128)}, u32[]{:S(2)}) copy-start(f32[128,128]{1,0:T(8,128)} %constant.23.clone.band_h) | copy-start | bytes 196612
  9.8 0.8 %copy-start.9 = (f32[120,120]{1,0:T(8,128)S(1)}, f32[120,120]{1,0:T(8,128)}, u32[]{:S(2)}) copy-start(f32[120,120]{1,0:T(8,128)} %c_ref.1) | copy-start | bytes 172804
  10.6 0.7 copy-start.10
where the time goes:
time: 76.3 us; the launch traced here: 75.8 us
  Pallas kernels  63.7 us (83%)
  local copies, waits for them, and re-layouts  12 us (16%)
    pallas_call x1, Pallas kernels, local(): pl.pallas_call(kernel, out_shape=jax.ShapeDtypeStruct((MOMENTS * OWN, LIN...  63.7 us
    unnamed x27, local copies, waits for them, and re-layouts  12 us

commit v1 on v0

--- a/solution.py
+++ b/solution.py
@@ -18,6 +18,7 @@
 LINES = 128
 OWN = 8
 LANES = 128
+STRIDE = 37
 MOMENTS = 120
 MASK_LANE = 120
 HALF = 72
@@ -63,6 +64,9 @@
     return roots
 
 
+SPEED = hermite_roots(DEG + 1)[-1]
+
+
 def coupling(entries, lookup, direction):
     matrix = np.zeros((LANES, LANES))
     for position, moment in enumerate(entries):
@@ -99,7 +103,7 @@
 
 def right_factor(table):
     high, low = parts(table)
-    return np.block([[high, low], [high, np.zeros_like(low)]])
+    return np.block([[high, low], [high, low]])
 
 
 @functools.cache
@@ -108,7 +112,6 @@
     lookup = {moment: position for position, moment in enumerate(entries)}
     values, modes = axial_modes(lookup)
     a2 = coupling(entries, lookup, 1)
-    speed = hermite_roots(DEG + 1)[-1]
     eye = np.eye(LANES)
 
     high, low = parts(modes.T)
@@ -122,7 +125,7 @@
     for own in range(OWN):
         phase = (((OWN * line + own)[:, None] * k1[None, :]) % NX) * (2 * math.pi / NX)
         cosine, sine = np.cos(phase) * used, np.sin(phase) * used
-        forward.append(np.concatenate(parts(np.concatenate([cosine.T, -sine.T], axis=0)), axis=1))
+        forward.append(np.concatenate(parts(np.concatenate([cosine.T, -sine.T], axis=0)), axis=0))
         inverse.append(np.concatenate(parts(np.concatenate([cosine * weight, -sine * weight], axis=1)), axis=0))
     forward, inverse = np.stack(forward), np.stack(inverse)
 
@@ -132,33 +135,40 @@
     series = np.stack([1 - angle**2 / 2 + angle**4 / 24, -(angle - angle**3 / 6)])
     series = series.astype(np.float32)
 
-    here = modes.T * (1 - CROSS_STEP * speed)
-    upper = modes.T @ (0.5 * CROSS_STEP * (speed * eye - a2))
-    lower = modes.T @ (0.5 * CROSS_STEP * (speed * eye + a2))
-    cross = np.stack(
-        [np.concatenate([right_factor(m) for m in order]) for order in ((here, upper, lower), (here, lower, upper))]
-    )
+    units = [lookup[1, 0, 0], lookup[0, 1, 0], lookup[0, 0, 1]]
+    combinations = [(0,), (1,), (2,), (0, 1), (0, 2), (1, 2)]
+    spare, target = eye.copy(), np.zeros((LANES, LANES))
+    for lane, group in enumerate(combinations, MOMENTS):
+        for d in group:
+            spare[units[d], lane] = 1.0
+    spare[MOMENTS:, MOMENTS:] = 0.0
+    for position, moment in enumerate(entries):
+        if sum(moment) == 2:
+            d = tuple(direction for direction in range(3) for _ in range(moment[direction]))
+            if d[0] == d[1]:
+                target[MOMENTS + d[0], position] = COLLIDE_STEP * ROOT_HALF
+            else:
+                target[MOMENTS + combinations.index(d), position] = 0.5 * COLLIDE_STEP
+                target[MOMENTS + d[0], position] = target[MOMENTS + d[1], position] = -0.5 * COLLIDE_STEP
+    cross = np.concatenate([right_factor(modes.T @ spare), right_factor(modes.T @ (-0.5 * CROSS_STEP * a2) @ spare)])
 
     degrees = np.array([sum(moment) for moment in entries] + [0] * (LANES - MOMENTS))
     band = (np.abs(degrees[:, None] - degrees[None, :]) <= 1) & (degrees[:, None] >= 2) & (degrees[None, :] >= 2)
-    first, second = np.zeros((LANES, LANES)), np.zeros((LANES, LANES))
-    rows = np.zeros((8, LANES), np.float32)
-    units = [lookup[1, 0, 0], lookup[0, 1, 0], lookup[0, 0, 1]]
-    for position, moment in enumerate(entries):
-        if sum(moment) == 2:
-            d = [direction for direction in range(3) for _ in range(moment[direction])]
-            first[units[d[0]], position] = 1.0
-            second[units[d[1]], position] = 1.0
-            rows[0, position] = COLLIDE_STEP * (ROOT_HALF if d[0] == d[1] else 1.0)
-    pick = np.concatenate([first, second], axis=1)
-    pick = np.concatenate([pick, pick], axis=0).astype(ml_dtypes.bfloat16)
-    rows[1] = COLLIDE_STEP * (degrees >= 2)
     band = (band * COLLIDE_STEP).astype(np.float32)
-    modes_right = right_factor(modes)
+    target = target.astype(np.float32)
+    relaxed = np.diag(COLLIDE_STEP * (degrees >= 2)).astype(np.float32)
+    square = np.stack([band, target - relaxed, np.diag(np.arange(LANES) < MOMENTS).astype(np.float32)])
+    high, low = parts(modes)
+    modes_right = np.concatenate([high, high, low], axis=0)
     return dict(
-        to_modes=to_modes, forward=forward, inverse=inverse, series=series, cross=cross, band=band, rows=rows, pick=pick,
-        modes_right=modes_right,
+        to_modes=to_modes, forward=forward, inverse=inverse, series=series, cross=cross, square=square, modes_right=modes_right,
     )
+
+
+def doubled(a):
+    high, low = split(a)
+    both = jnp.concatenate([high, low], axis=1)
+    return jnp.concatenate([both, both], axis=0)
 
 
 def split(a):
@@ -211,17 +221,17 @@
 
 
 def place_of(device):
-    core, y, x_hi, z = device % 2, (device // 2) % 4, (device // 8) % 2, device // 16
-    turn = z * 4 + y + (z % 2) * (3 - 2 * y)
+    core, y, x_hi, z = device & 1, (device >> 1) & 3, (device >> 3) & 1, device >> 4
+    turn = z * 4 + y + (z & 1) * (3 - 2 * y)
     return (x_hi * 32 + turn + x_hi * (31 - 2 * turn)) * 2 + core
 
 
 def kernel(
-    x_ref, mask_ref, c_ref, rate_ref,
-    to_modes_h, forward_h, inverse_h, series_h, cross_h, band_h, rows_h, pick_h, modes_h,
+    x_h, mask_h, c_h, rate_h,
+    to_modes_h, forward_h, inverse_h, series_h, cross_h, square_h, modes_h,
     out_ref,
-    to_modes, forward, inverse, series, cross, band, rows, pick, modes,
-    send1, recv1, send2, recv2, lines, beside, wall, spectrum, square, rate_row, collide,
+    x_ref, mask_ref, c_ref, rate_ref, to_modes, forward, inverse, series, cross, square, modes,
+    send1, recv1, send2, recv2, lines, beside, wall, spectrum, padded, rate_row, collide, advance_modes,
     table_sem, send_sem, recv_sem, edge_send, edge_recv, near_send, near_recv,
 ):
     me, slab = lax.axis_index("wa"), lax.axis_index("gy")
@@ -232,29 +242,33 @@
     is_first = 1 - (place + LINES - 1) // LINES
     prev_wa, prev_gy = device_at(place - 1 + is_first), slab + is_first * (1 - 2 * slab)
 
-    barrier = pltpu.get_barrier_semaphore()
-
-    @pl.loop(1, LINES)
-    def _(step):
-        pl.semaphore_signal(barrier, inc=1, device_id=((me + step) % LINES, slab), device_id_type=MESH)
-
-    pl.semaphore_signal(barrier, inc=1, device_id=(me, 1 - slab), device_id_type=MESH)
-
     loads = [
         pltpu.make_async_copy(src, dst, table_sem.at[i])
         for i, (src, dst) in enumerate(
-            [(to_modes_h, to_modes), (forward_h, forward), (series_h, series), (inverse_h, inverse), (cross_h.at[slab], cross.at[0]),
-             (cross_h.at[0], cross.at[1]), (band_h, band), (rows_h, rows), (pick_h, pick), (modes_h, modes)]
+            [(x_h, x_ref), (mask_h, mask_ref), (to_modes_h, to_modes), (c_h, c_ref), (rate_h, rate_ref), (forward_h, forward),
+             (series_h, series), (inverse_h, inverse), (cross_h, cross), (square_h, square), (modes_h, modes)]
         )
     ]
-    for load in loads:
+    for load in loads[:3]:
         load.start()
-    loads[0].wait()
+
+    barrier = pltpu.get_barrier_semaphore()
+
+    @pl.loop(1, LINES)
+    def _(step):
+        pl.semaphore_signal(barrier, inc=1, device_id=((me + step) & (LINES - 1), slab), device_id_type=MESH)
+
+    pl.semaphore_signal(barrier, inc=1, device_id=(me, 1 - slab), device_id_type=MESH)
+
+    for load in loads[3:]:
+        load.start()
+    for load in loads[:3]:
+        load.wait()
 
     row = lax.broadcasted_iota(jnp.int32, (LANES, LANES), 0)
     lane = lax.broadcasted_iota(jnp.int32, (LANES, LANES), 1)
 
-    @pl.loop(0, OWN)
+    @pl.loop(0, OWN, unroll=True)
     def _(own):
         cells = x_ref[pl.ds(own, MOMENTS, stride=OWN), :]
         cells = jnp.concatenate([cells, jnp.zeros((LANES - MOMENTS, LANES), F32)], axis=0)
@@ -268,7 +282,7 @@
 
     @pl.loop(1, LINES)
     def _(step):
-        target = (me + step) % LINES
+        target = (me + step * STRIDE) & (LINES - 1)
         target_place = place_of(target)
         target_line = target_place + slab * (LINES - 1 - 2 * target_place)
         pltpu.make_async_remote_copy(
@@ -282,33 +296,29 @@
 
     recv1[pl.ds(pl.multiple_of(me * OWN, OWN), OWN), :] = send1[pl.ds(pl.multiple_of(my_line * OWN, OWN), OWN), :]
 
-    for load in loads[1:]:
+    for load in loads[3:]:
         load.wait()
-    square[...] = jnp.zeros_like(square)
-    square[:MOMENTS, :MOMENTS] = c_ref[...]
+    padded[...] = jnp.zeros_like(padded)
+    padded[:MOMENTS, :MOMENTS] = c_ref[...]
     rate_row[...] = jnp.zeros_like(rate_row)
     rate_row[:, :MOMENTS] = rate_ref[...]
-    rates = rate_row[...] * rows[1:2, :]
-    linear = (square[...] * band[...]).T + jnp.where(row == lane, 1.0 - rates, 0.0)
+    linear = (padded[...] * square[0]).T + square[1] * rate_row[...] + square[2]
+    collide[...] = doubled(linear)
     high, low = split(linear)
-    collide[...] = jnp.concatenate(
-        [jnp.concatenate([high, low], axis=1), jnp.concatenate([high, jnp.zeros_like(low)], axis=1)], axis=0
-    )
-    drive = rate_row[...] * rows[0:1, :]
-
-    def finish(here, after, before, factor, keep):
-        operand = jnp.concatenate([*split(here), *split(after), *split(before)], axis=1)
-        f = fold(jnp.dot(operand, factor, preferred_element_type=F32)) * keep
-        operand = jnp.concatenate(split(f), axis=1)
-        mixed = fold(jnp.dot(operand, collide[...], preferred_element_type=F32))
-        chosen = jnp.dot(operand, pick[...], preferred_element_type=F32)
-        return mixed + drive * (chosen[:, :LANES] * chosen[:, LANES:])
+    linear = jnp.dot(jnp.concatenate([high, low, high], axis=1), modes[...], preferred_element_type=F32)
+    advance_modes[...] = doubled(linear)
+
+    def finish(here, sums, differences, keep, factor):
+        here = here * (1 - CROSS_STEP * SPEED) + sums * (0.5 * CROSS_STEP * SPEED)
+        operand = jnp.concatenate([*split(here), *split(differences)], axis=1)
+        f = fold(jnp.dot(operand, cross[...], preferred_element_type=F32)) * keep
+        f = jnp.where(lax.broadcasted_iota(jnp.int32, f.shape, 1) >= MOMENTS, f * f, f)
+        return fold(jnp.dot(jnp.concatenate(split(f), axis=1), factor[...], preferred_element_type=F32))
 
     def to_spectrum(own, cells):
-        high, low = split(cells)
         table = forward[own]
-        operand = jnp.concatenate([table[:, :LANES], table], axis=1)
-        spectrum[own] = jnp.dot(operand, jnp.concatenate([high, low, high], axis=0), preferred_element_type=F32)
+        both = jnp.dot(jnp.concatenate([table, table], axis=1), jnp.concatenate(split(cells), axis=0), preferred_element_type=F32)
+        spectrum[own] = both[: 2 * HALF] + both[2 * HALF :]
 
     def advance():
         @pl.loop(0, BLOCKS)
@@ -325,15 +335,13 @@
                 spectrum[own, im, :] = ui
 
     def from_spectrum(own):
-        high, low = split(spectrum[own])
-        table = inverse[own]
-        main = jnp.dot(table[:LINES], jnp.concatenate([high, low], axis=1), preferred_element_type=F32)
-        return fold(main) + jnp.dot(table[LINES:], high, preferred_element_type=F32)
+        both = fold(jnp.dot(inverse[own], jnp.concatenate(split(spectrum[own]), axis=1), preferred_element_type=F32))
+        return both[:LINES] + both[LINES:]
 
     rest = pl.ds(0, (LINES - 1) * OWN)
     pltpu.make_async_copy(recv1.at[rest, :], recv1.at[rest, :], recv_sem.at[0]).wait()
 
-    @pl.loop(0, OWN)
+    @pl.loop(0, OWN, unroll=True)
     def _(own):
         cells = recv1[pl.ds(own, LINES, stride=OWN), :]
         flags = jnp.broadcast_to(cells[:, MASK_LANE : MASK_LANE + 1], (LINES, LANES))
@@ -353,25 +361,25 @@
             device_id_type=MESH,
         )
 
-    @pl.loop(0, OWN)
+    @pl.loop(0, OWN, unroll=True)
     def _(own):
         lines[own] = from_spectrum(own)
         near(own, 0).start()
         near(own, 1).start()
 
     inside = 1.0 - is_first.astype(F32)
-
-    @pl.loop(0, OWN)
+    upward = 1.0 - 2.0 * slab.astype(F32)
+
+    @pl.loop(0, OWN, unroll=True)
     def _(own):
         for slot in range(2):
             pltpu.make_async_copy(lines.at[own], beside.at[slot, own], near_recv.at[slot, own]).wait()
-        f = finish(lines[own], beside[1, own], beside[0, own] * inside, cross[0], wall[own])
-        f = fold(jnp.dot(jnp.concatenate(split(f), axis=1), modes[...], preferred_element_type=F32))
-        to_spectrum(own, f)
+        after, before = beside[1, own], beside[0, own] * inside
+        to_spectrum(own, finish(lines[own], after + before, (after - before) * upward, wall[own], advance_modes))
 
     advance()
 
-    @pl.loop(0, OWN)
+    @pl.loop(0, OWN, unroll=True)
     def _(own):
         send2[pl.ds(own, LINES, stride=OWN), :] = from_spectrum(own)
 
@@ -379,7 +387,7 @@
 
     @pl.loop(1, LINES)
     def _(step):
-        target = (me + step) % LINES
+        target = (me + step * STRIDE) & (LINES - 1)
         pltpu.make_async_remote_copy(
             src_ref=send2.at[pl.ds(pl.multiple_of(target * OWN, OWN), OWN), :],
             dst_ref=recv2.at[my_tile, :],
@@ -421,20 +429,17 @@
 
     beyond.wait()
 
-    @pl.loop(0, OWN)
+    @pl.loop(0, OWN, unroll=True)
     def _(own):
         flags = send1[pl.ds(own, LINES, stride=OWN), :][:, MASK_LANE : MASK_LANE + 1]
         keep = jnp.where(lane == 0, 1.0, 1.0 - jnp.broadcast_to(flags, (LINES, LANES)))
-        f = finish(
-            recv2[pl.ds(OWN + own, LINES, stride=OWN), :],
-            recv2[pl.ds(2 * OWN + own, LINES, stride=OWN), :],
-            recv2[pl.ds(own, LINES, stride=OWN), :],
-            cross[1],
-            keep,
-        )
+        here = recv2[pl.ds(OWN + own, LINES, stride=OWN), :]
+        after = recv2[pl.ds(2 * OWN + own, LINES, stride=OWN), :]
+        before = recv2[pl.ds(own, LINES, stride=OWN), :]
+        f = finish(here, after + before, after - before, keep, collide)
         out_ref[pl.ds(own, MOMENTS, stride=OWN), :] = f.T[:MOMENTS]
 
-    @pl.loop(0, OWN)
+    @pl.loop(0, OWN, unroll=True)
     def _(own):
         near(own, 0).wait_send()
         near(own, 1).wait_send()
@@ -445,22 +450,29 @@
 
 def local(moments, mask, coefficients, rates):
     t = tables()
-    names = ["to_modes", "forward", "inverse", "series", "cross", "band", "rows", "pick", "modes_right"]
+    names = ["to_modes", "forward", "inverse", "series", "cross", "square", "modes_right"]
     constants = [jnp.asarray(t[name]) for name in names]
     in_vmem = pl.BlockSpec(memory_space=pltpu.VMEM)
-    anywhere = pl.BlockSpec(memory_space=pl.ANY)
+    in_hbm = pl.BlockSpec(memory_space=pltpu.HBM)
     tile = (NX, LANES)
     line = (OWN, LINES, LANES)
     out = pl.pallas_call(
         kernel,
         out_shape=jax.ShapeDtypeStruct((MOMENTS * OWN, LINES), F32),
-        in_specs=[in_vmem] * 4 + [anywhere] * len(constants),
+        in_specs=[in_hbm] * (4 + len(constants)),
         out_specs=in_vmem,
-        scratch_shapes=[pltpu.VMEM(c.shape, c.dtype) for c in constants]
+        scratch_shapes=[
+            pltpu.VMEM((MOMENTS * OWN, LINES), F32),
+            pltpu.VMEM((OWN, LINES), jnp.int32),
+            pltpu.VMEM((MOMENTS, MOMENTS), F32),
+            pltpu.VMEM((1, MOMENTS), F32),
+        ]
+        + [pltpu.VMEM(c.shape, c.dtype) for c in constants]
         + [pltpu.VMEM(shape, F32) for shape in (tile, tile, tile, (NX + 2 * OWN, LANES), line, (2, *line), line, (OWN, 2 * HALF, LANES), (LANES, LANES), (1, LANES))]
         + [
             pltpu.VMEM((2 * LANES, 2 * LANES), BF16),
-            pltpu.SemaphoreType.DMA((10,)),
+            pltpu.VMEM((2 * LANES, 2 * LANES), BF16),
+            pltpu.SemaphoreType.DMA((11,)),
             pltpu.SemaphoreType.DMA((2,)),
             pltpu.SemaphoreType.DMA((3,)),
             pltpu.SemaphoreType.DMA,
@@ -468,7 +480,7 @@
             pltpu.SemaphoreType.DMA((2, OWN)),
             pltpu.SemaphoreType.DMA((2, OWN)),
         ],
-        compiler_params=pltpu.CompilerParams(collective_id=0, has_side_effects=True, vmem_limit_bytes=48 * 1024 * 1024),
+        compiler_params=pltpu.CompilerParams(collective_id=0, has_side_effects=True, vmem_limit_bytes=62 * 1024 * 1024),
         name="duct",
     )(
         moments.reshape(MOMENTS * OWN, LINES),

time: 76.3 us -> 61.3 us (0.80)
  local copies, waits for them, and re-layouts: 12 us -> 1.84 us
  Pallas kernels: 63.7 us -> 59.4 us
    unnamed x27 -> x1, local copies, waits for them, and re-layouts: 12 us -> 1.84 us
    pallas_call x1, Pallas kernels: 63.7 us -> 59.4 us  [local(): pl.pallas_call(kernel, out_shape=jax.ShapeDtypeStruct((MOMENTS * OWN, LIN...]
where the time goes in v1:
time: 61.3 us; the launch traced here: 61.2 us
  Pallas kernels  59.4 us (97%)
  local copies, waits for them, and re-layouts  1.84 us (3%)
    pallas_call x1, Pallas kernels, local(): pl.pallas_call(kernel, out_shape=jax.ShapeDtypeStruct((MOMENTS * OWN, LIN...  59.4 us
    unnamed x1, local copies, waits for them, and re-layouts  1.84 us

profile of v1, /device:TPU:1, one launch (start us, length us, event | category | flops | bytes accessed | tf_op | source)
XLA Modules:
  0.0 61.2 jit_solution(8952655180603110719)
XLA Ops:
  0.0 59.4 %duct.1 = f32[960,128]{1,0:T(8,128)} custom-call(f32[960,128]{1,0:T(8,128)} %bitcast.4, s32[8,128]{1,0:T(8,128)} %mask_h.1, f32[120,120]{1,0:T(8,128)} %c_h.1, f32[1,120]{1,0:T(1,128)} %bitcast.5, bf16[128,384]{1,0:T(8,128)(2,1)} %constant.14.clone.to_modes_h, bf16[8,288,128]{2,1,0:T(8,128)(2,1)} %constant.15.clone.forward_h, ...), custom_call_target="tpu_custom_call" | custom-call | tf_op jit(solution)/shard_map/duct/pallas_call | solution.py:459
  59.4 1.8 %copy.13 = f32[120,8,128]{2,1,0:T(8,128)} copy(f32[120,8,128]{2,1,0:T(8,128)} %bitcast.3) | data formatting | bytes 983040

commit v2 on v1

--- a/solution.py
+++ b/solution.py
@@ -18,6 +18,8 @@
 LINES = 128
 OWN = 8
 LANES = 128
+DISTANCES = (1, 7, 2, 6, 3, 5, 4, 0)
+PLANE = 16
 STRIDE = 37
 MOMENTS = 120
 MASK_LANE = 120
@@ -126,7 +128,8 @@
         phase = (((OWN * line + own)[:, None] * k1[None, :]) % NX) * (2 * math.pi / NX)
         cosine, sine = np.cos(phase) * used, np.sin(phase) * used
         forward.append(np.concatenate(parts(np.concatenate([cosine.T, -sine.T], axis=0)), axis=0))
-        inverse.append(np.concatenate(parts(np.concatenate([cosine * weight, -sine * weight], axis=1)), axis=0))
+        high, low = parts(np.concatenate([cosine * weight, -sine * weight], axis=1))
+        inverse.append(np.concatenate([high, high, low], axis=1))
     forward, inverse = np.stack(forward), np.stack(inverse)
 
     wave = k1[None, :] + 128 * np.arange(8)[:, None]
@@ -231,8 +234,8 @@
     to_modes_h, forward_h, inverse_h, series_h, cross_h, square_h, modes_h,
     out_ref,
     x_ref, mask_ref, c_ref, rate_ref, to_modes, forward, inverse, series, cross, square, modes,
-    send1, recv1, send2, recv2, lines, beside, wall, spectrum, padded, rate_row, collide, advance_modes,
-    table_sem, send_sem, recv_sem, edge_send, edge_recv, near_send, near_recv,
+    send1, recv1, send2, recv2, beside, wall, pair, spectrum, padded, rate_row, collide, advance_modes,
+    table_sem, send_sem, plane_recv, recv_sem, edge_send, edge_recv, near_send, near_recv,
 ):
     me, slab = lax.axis_index("wa"), lax.axis_index("gy")
     place = place_of(me)
@@ -280,19 +283,23 @@
 
     pl.semaphore_wait(barrier, LINES)
 
-    @pl.loop(1, LINES)
-    def _(step):
-        target = (me + step * STRIDE) & (LINES - 1)
-        target_place = place_of(target)
-        target_line = target_place + slab * (LINES - 1 - 2 * target_place)
-        pltpu.make_async_remote_copy(
-            src_ref=send1.at[pl.ds(pl.multiple_of(target_line * OWN, OWN), OWN), :],
-            dst_ref=recv1.at[pl.ds(pl.multiple_of(me * OWN, OWN), OWN), :],
-            send_sem=send_sem.at[0],
-            recv_sem=recv_sem.at[0],
-            device_id=(target, slab),
-            device_id_type=MESH,
-        ).start()
+    z = me >> 4
+
+    for distance in DISTANCES:
+
+        @pl.loop(0 if distance else 1, PLANE)
+        def _(step):
+            target = ((z + distance) & 7) * PLANE + ((me + step) & (PLANE - 1))
+            target_place = place_of(target)
+            target_line = target_place + slab * (LINES - 1 - 2 * target_place)
+            pltpu.make_async_remote_copy(
+                src_ref=send1.at[pl.ds(pl.multiple_of(target_line * OWN, OWN), OWN), :],
+                dst_ref=recv1.at[pl.ds(pl.multiple_of(me * OWN, OWN), OWN), :],
+                send_sem=send_sem.at[0],
+                recv_sem=plane_recv.at[z],
+                device_id=(target, slab),
+                device_id_type=MESH,
+            ).start()
 
     recv1[pl.ds(pl.multiple_of(me * OWN, OWN), OWN), :] = send1[pl.ds(pl.multiple_of(my_line * OWN, OWN), OWN), :]
 
@@ -308,80 +315,92 @@
     linear = jnp.dot(jnp.concatenate([high, low, high], axis=1), modes[...], preferred_element_type=F32)
     advance_modes[...] = doubled(linear)
 
-    def finish(here, sums, differences, keep, factor):
-        here = here * (1 - CROSS_STEP * SPEED) + sums * (0.5 * CROSS_STEP * SPEED)
-        operand = jnp.concatenate([*split(here), *split(differences)], axis=1)
-        f = fold(jnp.dot(operand, cross[...], preferred_element_type=F32)) * keep
-        f = jnp.where(lax.broadcasted_iota(jnp.int32, f.shape, 1) >= MOMENTS, f * f, f)
-        return fold(jnp.dot(jnp.concatenate(split(f), axis=1), factor[...], preferred_element_type=F32))
+    def beside_terms(here, after, before):
+        return here * (1 - CROSS_STEP * SPEED) + (after + before) * (0.5 * CROSS_STEP * SPEED), after - before
+
+    def finish(fields, keeps, factor):
+        moved = []
+        for (here, differences), keep in zip(fields, keeps):
+            operand = jnp.concatenate([*split(here), *split(differences)], axis=1)
+            moved.append(fold(jnp.dot(operand, cross[...], preferred_element_type=F32)) * keep())
+        moved = [jnp.where(lane >= MOMENTS, f * f, f) for f in moved]
+        return [fold(jnp.dot(jnp.concatenate(split(f), axis=1), factor[...], preferred_element_type=F32)) for f in moved]
 
     def to_spectrum(own, cells):
         table = forward[own]
         both = jnp.dot(jnp.concatenate([table, table], axis=1), jnp.concatenate(split(cells), axis=0), preferred_element_type=F32)
-        spectrum[own] = both[: 2 * HALF] + both[2 * HALF :]
-
-    def advance():
+        return both[: 2 * HALF] + both[2 * HALF :]
+
+    def advance(spectrum, start):
+        lanes = pl.ds(start, LANES)
+
         @pl.loop(0, BLOCKS)
         def _(block):
             at = pl.multiple_of(block * 8, 8)
             re, im = pl.ds(at, 8), pl.ds(pl.multiple_of(HALF + at, 8), 8)
-            f = fourier8([(spectrum[own, re, :], spectrum[own, im, :]) for own in range(OWN)], -1)
+            f = fourier8([(spectrum[own, re, lanes], spectrum[own, im, lanes]) for own in range(OWN)], -1)
             h = []
             for k, (fr, fi) in enumerate(f):
                 pr, pi = series[0, k, re, :], series[1, k, re, :]
                 h.append((pr * fr - pi * fi, pr * fi + pi * fr))
             for own, (ur, ui) in enumerate(fourier8(h, 1)):
-                spectrum[own, re, :] = ur
-                spectrum[own, im, :] = ui
-
-    def from_spectrum(own):
-        both = fold(jnp.dot(inverse[own], jnp.concatenate(split(spectrum[own]), axis=1), preferred_element_type=F32))
-        return both[:LINES] + both[LINES:]
-
-    rest = pl.ds(0, (LINES - 1) * OWN)
-    pltpu.make_async_copy(recv1.at[rest, :], recv1.at[rest, :], recv_sem.at[0]).wait()
-
-    @pl.loop(0, OWN, unroll=True)
-    def _(own):
-        cells = recv1[pl.ds(own, LINES, stride=OWN), :]
-        flags = jnp.broadcast_to(cells[:, MASK_LANE : MASK_LANE + 1], (LINES, LANES))
-        wall[own] = jnp.where(lane == 0, 1.0, 1.0 - flags)
-        to_spectrum(own, cells)
-
-    advance()
-
-    def near(own, which):
+                spectrum[own, re, lanes] = ur
+                spectrum[own, im, lanes] = ui
+
+    def from_spectrum(own, values):
+        high, low = split(values)
+        return jnp.dot(inverse[own], jnp.concatenate([high, low, high], axis=0), preferred_element_type=F32)
+
+    def near(plane, which):
         slot = 1 - is_first if which else is_edge
+        part = pl.ds(pl.multiple_of(plane * (PLANE * OWN), PLANE * OWN), PLANE * OWN)
         return pltpu.make_async_remote_copy(
-            src_ref=lines.at[own],
-            dst_ref=beside.at[slot, own],
-            send_sem=near_send.at[which, own],
-            recv_sem=near_recv.at[slot, own],
+            src_ref=recv1.at[part, :],
+            dst_ref=beside.at[slot, part, :],
+            send_sem=near_send.at[which, plane],
+            recv_sem=near_recv.at[slot, plane],
             device_id=(prev_wa, prev_gy) if which else (next_wa, next_gy),
             device_id_type=MESH,
         )
 
+    for distance in DISTANCES:
+        plane = (z - distance) & 7
+        part = pl.ds(0, (PLANE if distance else PLANE - 1) * OWN)
+        pltpu.make_async_copy(recv1.at[part, :], recv1.at[part, :], plane_recv.at[plane]).wait()
+        near(plane, 0).start()
+        near(plane, 1).start()
+
+    @pl.loop(0, OWN)
+    def _(plane):
+        part = pl.ds(pl.multiple_of(plane * (PLANE * OWN), PLANE * OWN), PLANE * OWN)
+        for slot in range(2):
+            pltpu.make_async_copy(recv1.at[part, :], beside.at[slot, part, :], near_recv.at[slot, plane]).wait()
+
+    inside = 1.0 - is_first.astype(F32)
+    upward = 1.0 - 2.0 * slab.astype(F32)
+
     @pl.loop(0, OWN, unroll=True)
     def _(own):
-        lines[own] = from_spectrum(own)
-        near(own, 0).start()
-        near(own, 1).start()
-
-    inside = 1.0 - is_first.astype(F32)
-    upward = 1.0 - 2.0 * slab.astype(F32)
+        rows = pl.ds(own, LINES, stride=OWN)
+        cells = recv1[rows, :]
+        flags = jnp.broadcast_to(cells[:, MASK_LANE : MASK_LANE + 1], (LINES, LANES))
+        wall[own] = jnp.where(lane == 0, 1.0, 1.0 - flags)
+        here, differences = beside_terms(cells, beside[1, rows, :], beside[0, rows, :] * inside)
+        pair[own] = to_spectrum(own, jnp.concatenate([here, differences * upward], axis=1))
+
+    advance(pair, 0)
+    advance(pair, LANES)
+
+    fields = [from_spectrum(own, pair[own]) for own in range(OWN)]
+    fields = [(f[:, :LANES], f[:, LANES:]) for f in fields]
+    for own, f in enumerate(finish(fields, [functools.partial(wall.__getitem__, own) for own in range(OWN)], advance_modes)):
+        spectrum[own] = to_spectrum(own, f)
+
+    advance(spectrum, 0)
 
     @pl.loop(0, OWN, unroll=True)
     def _(own):
-        for slot in range(2):
-            pltpu.make_async_copy(lines.at[own], beside.at[slot, own], near_recv.at[slot, own]).wait()
-        after, before = beside[1, own], beside[0, own] * inside
-        to_spectrum(own, finish(lines[own], after + before, (after - before) * upward, wall[own], advance_modes))
-
-    advance()
-
-    @pl.loop(0, OWN, unroll=True)
-    def _(own):
-        send2[pl.ds(own, LINES, stride=OWN), :] = from_spectrum(own)
+        send2[pl.ds(own, LINES, stride=OWN), :] = from_spectrum(own, spectrum[own])
 
     my_tile = pl.ds(pl.multiple_of((my_line + 1) * OWN, OWN), OWN)
 
@@ -392,7 +411,7 @@
             src_ref=send2.at[pl.ds(pl.multiple_of(target * OWN, OWN), OWN), :],
             dst_ref=recv2.at[my_tile, :],
             send_sem=send_sem.at[1],
-            recv_sem=recv_sem.at[1 + is_edge],
+            recv_sem=recv_sem.at[is_edge],
             device_id=(target, slab),
             device_id_type=MESH,
         ).start()
@@ -403,10 +422,12 @@
 
     edge_tile = pl.ds(pl.multiple_of((LINES - slab * (LINES - 1)) * OWN, OWN), OWN)
 
+    rest = pl.ds(0, (LINES - 1) * OWN)
+
     @pl.when(is_edge == 0)
     def _():
         one = pl.ds(0, OWN)
-        pltpu.make_async_copy(recv2.at[one, :], recv2.at[one, :], recv_sem.at[2]).wait()
+        pltpu.make_async_copy(recv2.at[one, :], recv2.at[one, :], recv_sem.at[1]).wait()
 
     beyond = pltpu.make_async_remote_copy(
         src_ref=recv2.at[edge_tile, :],
@@ -420,29 +441,30 @@
 
     @pl.when(is_edge == 1)
     def _():
-        pltpu.make_async_copy(recv2.at[rest, :], recv2.at[rest, :], recv_sem.at[1]).wait()
+        pltpu.make_async_copy(recv2.at[rest, :], recv2.at[rest, :], recv_sem.at[0]).wait()
 
     @pl.when(is_edge == 0)
     def _():
         less = pl.ds(0, (LINES - 2) * OWN)
-        pltpu.make_async_copy(recv2.at[less, :], recv2.at[less, :], recv_sem.at[1]).wait()
+        pltpu.make_async_copy(recv2.at[less, :], recv2.at[less, :], recv_sem.at[0]).wait()
 
     beyond.wait()
 
-    @pl.loop(0, OWN, unroll=True)
-    def _(own):
+    def keep_here(own):
         flags = send1[pl.ds(own, LINES, stride=OWN), :][:, MASK_LANE : MASK_LANE + 1]
-        keep = jnp.where(lane == 0, 1.0, 1.0 - jnp.broadcast_to(flags, (LINES, LANES)))
-        here = recv2[pl.ds(OWN + own, LINES, stride=OWN), :]
-        after = recv2[pl.ds(2 * OWN + own, LINES, stride=OWN), :]
-        before = recv2[pl.ds(own, LINES, stride=OWN), :]
-        f = finish(here, after + before, after - before, keep, collide)
+        return jnp.where(lane == 0, 1.0, 1.0 - jnp.broadcast_to(flags, (LINES, LANES)))
+
+    fields = []
+    for own in range(OWN):
+        before, here, after = (recv2[pl.ds(tile * OWN + own, LINES, stride=OWN), :] for tile in range(3))
+        fields.append(beside_terms(here, after, before))
+    for own, f in enumerate(finish(fields, [functools.partial(keep_here, own) for own in range(OWN)], collide)):
         out_ref[pl.ds(own, MOMENTS, stride=OWN), :] = f.T[:MOMENTS]
 
-    @pl.loop(0, OWN, unroll=True)
-    def _(own):
-        near(own, 0).wait_send()
-        near(own, 1).wait_send()
+    @pl.loop(0, OWN)
+    def _(plane):
+        near(plane, 0).wait_send()
+        near(plane, 1).wait_send()
 
     pltpu.make_async_copy(send1.at[rest, :], send1.at[rest, :], send_sem.at[0]).wait()
     pltpu.make_async_copy(send2.at[rest, :], send2.at[rest, :], send_sem.at[1]).wait()
@@ -468,13 +490,17 @@
             pltpu.VMEM((1, MOMENTS), F32),
         ]
         + [pltpu.VMEM(c.shape, c.dtype) for c in constants]
-        + [pltpu.VMEM(shape, F32) for shape in (tile, tile, tile, (NX + 2 * OWN, LANES), line, (2, *line), line, (OWN, 2 * HALF, LANES), (LANES, LANES), (1, LANES))]
+        + [pltpu.VMEM(shape, F32) for shape in (
+            tile, tile, tile, (NX + 2 * OWN, LANES), (2, *tile), line, (OWN, 2 * HALF, 2 * LANES), (OWN, 2 * HALF, LANES),
+            (LANES, LANES), (1, LANES),
+        )]
         + [
             pltpu.VMEM((2 * LANES, 2 * LANES), BF16),
             pltpu.VMEM((2 * LANES, 2 * LANES), BF16),
             pltpu.SemaphoreType.DMA((11,)),
             pltpu.SemaphoreType.DMA((2,)),
-            pltpu.SemaphoreType.DMA((3,)),
+            pltpu.SemaphoreType.DMA((8,)),
+            pltpu.SemaphoreType.DMA((2,)),
             pltpu.SemaphoreType.DMA,
             pltpu.SemaphoreType.DMA,
             pltpu.SemaphoreType.DMA((2, OWN)),

time: 61.3 us -> 59 us (0.962)
  Pallas kernels: 59.4 us -> 57 us
    pallas_call x1, Pallas kernels: 59.4 us -> 57 us  [local(): pl.pallas_call(kernel, out_shape=jax.ShapeDtypeStruct((MOMENTS * OWN, LIN...]
where the time goes in v2:
time: 59 us; the launch traced here: 58.9 us
  Pallas kernels  57 us (97%)
  local copies, waits for them, and re-layouts  1.84 us (3%)
    pallas_call x1, Pallas kernels, local(): pl.pallas_call(kernel, out_shape=jax.ShapeDtypeStruct((MOMENTS * OWN, LIN...  57 us
    unnamed x1, local copies, waits for them, and re-layouts  1.84 us

profile of v2, /device:TPU:1, one launch (start us, length us, event | category | flops | bytes accessed | tf_op | source)
XLA Modules:
  0.0 58.9 jit_solution(5834918174357309197)
XLA Ops:
  0.0 57.0 %duct.1 = f32[960,128]{1,0:T(8,128)} custom-call(f32[960,128]{1,0:T(8,128)} %bitcast.4, s32[8,128]{1,0:T(8,128)} %mask_h.1, f32[120,120]{1,0:T(8,128)} %c_h.1, f32[1,120]{1,0:T(1,128)} %bitcast.5, bf16[128,384]{1,0:T(8,128)(2,1)} %constant.14.clone.to_modes_h, bf16[8,288,128]{2,1,0:T(8,128)(2,1)} %constant.15.clone.forward_h, ...), custom_call_target="tpu_custom_call" | custom-call | tf_op jit(solution)/shard_map/duct/pallas_call | solution.py:481
  57.0 1.8 %copy.13 = f32[120,8,128]{2,1,0:T(8,128)} copy(f32[120,8,128]{2,1,0:T(8,128)} %bitcast.3) | data formatting | bytes 983040

commit v3 on v2

--- a/solution.py
+++ b/solution.py
@@ -18,7 +18,7 @@
 LINES = 128
 OWN = 8
 LANES = 128
-DISTANCES = (1, 7, 2, 6, 3, 5, 4, 0)
+DISTANCES = (4, 0, 3, 5, 2, 6, 1, 7)
 PLANE = 16
 STRIDE = 37
 MOMENTS = 120
@@ -257,7 +257,7 @@
 
     barrier = pltpu.get_barrier_semaphore()
 
-    @pl.loop(1, LINES)
+    @pl.loop(1, LINES, unroll=8)
     def _(step):
         pl.semaphore_signal(barrier, inc=1, device_id=((me + step) & (LINES - 1), slab), device_id_type=MESH)
 
@@ -285,21 +285,32 @@
 
     z = me >> 4
 
-    for distance in DISTANCES:
-
-        @pl.loop(0 if distance else 1, PLANE)
+    def serve1(target):
+        target_place = place_of(target)
+        target_line = target_place + slab * (LINES - 1 - 2 * target_place)
+        pltpu.make_async_remote_copy(
+            src_ref=send1.at[pl.ds(pl.multiple_of(target_line * OWN, OWN), OWN), :],
+            dst_ref=recv1.at[pl.ds(pl.multiple_of(me * OWN, OWN), OWN), :],
+            send_sem=send_sem.at[0],
+            recv_sem=plane_recv.at[z],
+            device_id=(target, slab),
+            device_id_type=MESH,
+        ).start()
+
+    for first in range(0, 8, 2):
+        pair_of = DISTANCES[first : first + 2]
+
+        @pl.loop(0, PLANE)
         def _(step):
-            target = ((z + distance) & 7) * PLANE + ((me + step) & (PLANE - 1))
-            target_place = place_of(target)
-            target_line = target_place + slab * (LINES - 1 - 2 * target_place)
-            pltpu.make_async_remote_copy(
-                src_ref=send1.at[pl.ds(pl.multiple_of(target_line * OWN, OWN), OWN), :],
-                dst_ref=recv1.at[pl.ds(pl.multiple_of(me * OWN, OWN), OWN), :],
-                send_sem=send_sem.at[0],
-                recv_sem=plane_recv.at[z],
-                device_id=(target, slab),
-                device_id_type=MESH,
-            ).start()
+            for distance in pair_of:
+                if distance:
+                    serve1(((z + distance) & 7) * PLANE + ((me + step) & (PLANE - 1)))
+
+        if 0 in pair_of:
+
+            @pl.loop(1, PLANE)
+            def _(step):
+                serve1(z * PLANE + ((me + step) & (PLANE - 1)))
 
     recv1[pl.ds(pl.multiple_of(me * OWN, OWN), OWN), :] = send1[pl.ds(pl.multiple_of(my_line * OWN, OWN), OWN), :]
 
@@ -406,7 +417,7 @@
 
     @pl.loop(1, LINES)
     def _(step):
-        target = (me + step * STRIDE) & (LINES - 1)
+        target = (me + ((step + 1) >> 1) * (STRIDE * (2 * (step & 1) - 1))) & (LINES - 1)
         pltpu.make_async_remote_copy(
             src_ref=send2.at[pl.ds(pl.multiple_of(target * OWN, OWN), OWN), :],
             dst_ref=recv2.at[my_tile, :],
@@ -480,7 +491,7 @@
     line = (OWN, LINES, LANES)
     out = pl.pallas_call(
         kernel,
-        out_shape=jax.ShapeDtypeStruct((MOMENTS * OWN, LINES), F32),
+        out_shape=pltpu.VMEM((MOMENTS * OWN, LINES), F32),
         in_specs=[in_hbm] * (4 + len(constants)),
         out_specs=in_vmem,
         scratch_shapes=[

time: 59 us -> 54.3 us (0.920)
  Pallas kernels: 57 us -> 53.3 us
  local copies, waits for them, and re-layouts: 1.84 us -> 0.78 us
    pallas_call x1, Pallas kernels: 57 us -> 53.3 us  [local(): pl.pallas_call(kernel, out_shape=pltpu.VMEM((MOMENTS * OWN, LINES), F32),...]
    unnamed x1, local copies, waits for them, and re-layouts: 1.84 us -> 0.78 us
where the time goes in v3:
time: 54.3 us; the launch traced here: 54.1 us
  Pallas kernels  53.3 us (98%)
  local copies, waits for them, and re-layouts  0.78 us (1%)
    pallas_call x1, Pallas kernels, local(): pl.pallas_call(kernel, out_shape=pltpu.VMEM((MOMENTS * OWN, LINES), F32),...  53.3 us

profile of v3, /device:TPU:1, one launch (start us, length us, event | category | flops | bytes accessed | tf_op | source)
XLA Modules:
  0.0 54.1 jit_solution(3402027784018010325)
XLA Ops:
  0.0 53.3 %duct.1 = f32[960,128]{1,0:T(8,128)S(1)} custom-call(f32[960,128]{1,0:T(8,128)} %bitcast.4, s32[8,128]{1,0:T(8,128)} %mask_h.1, f32[120,120]{1,0:T(8,128)} %c_h.1, f32[1,120]{1,0:T(1,128)} %bitcast.5, bf16[128,384]{1,0:T(8,128)(2,1)} %constant.14.clone.to_modes_h, bf16[8,288,128]{2,1,0:T(8,128)(2,1)} %constant.15.clone.forward_h, ...), custom_call_target="tpu_custom_call" | custom-call | tf_op jit(solution)/shard_map/duct/pallas_call | solution.py:492
  53.3 0.8 %copy.13 = f32[120,8,128]{2,1,0:T(8,128)} copy(f32[120,8,128]{2,1,0:T(8,128)S(1)} %bitcast.3) | data formatting | bytes 983040

commit v4 on v3

--- a/solution.py
+++ b/solution.py
@@ -271,15 +271,15 @@
     row = lax.broadcasted_iota(jnp.int32, (LANES, LANES), 0)
     lane = lax.broadcasted_iota(jnp.int32, (LANES, LANES), 1)
 
-    @pl.loop(0, OWN, unroll=True)
-    def _(own):
+    turned = []
+    for own in range(OWN):
         cells = x_ref[pl.ds(own, MOMENTS, stride=OWN), :]
         cells = jnp.concatenate([cells, jnp.zeros((LANES - MOMENTS, LANES), F32)], axis=0)
         high, low = split(cells)
-        turned = jnp.dot(to_modes[...], jnp.concatenate([high, low, high], axis=0), preferred_element_type=F32)
+        turned.append(jnp.dot(to_modes[...], jnp.concatenate([high, low, high], axis=0), preferred_element_type=F32))
+    for own in range(OWN):
         flags = mask_ref[pl.ds(own, 1), :].astype(F32)
-        turned = jnp.where(row == MASK_LANE, flags, turned)
-        send1[pl.ds(own, LINES, stride=OWN), :] = turned.T
+        send1[pl.ds(own, LINES, stride=OWN), :] = jnp.where(row == MASK_LANE, flags, turned[own]).T
 
     pl.semaphore_wait(barrier, LINES)
 
@@ -345,7 +345,7 @@
     def advance(spectrum, start):
         lanes = pl.ds(start, LANES)
 
-        @pl.loop(0, BLOCKS)
+        @pl.loop(0, BLOCKS, unroll=3)
         def _(block):
             at = pl.multiple_of(block * 8, 8)
             re, im = pl.ds(at, 8), pl.ds(pl.multiple_of(HALF + at, 8), 8)
@@ -381,6 +381,10 @@
         near(plane, 0).start()
         near(plane, 1).start()
 
+    for own in range(OWN):
+        flags = recv1[pl.ds(own, LINES, stride=OWN), :][:, MASK_LANE : MASK_LANE + 1]
+        wall[own] = jnp.where(lane == 0, 1.0, 1.0 - jnp.broadcast_to(flags, (LINES, LANES)))
+
     @pl.loop(0, OWN)
     def _(plane):
         part = pl.ds(pl.multiple_of(plane * (PLANE * OWN), PLANE * OWN), PLANE * OWN)
@@ -390,14 +394,14 @@
     inside = 1.0 - is_first.astype(F32)
     upward = 1.0 - 2.0 * slab.astype(F32)
 
-    @pl.loop(0, OWN, unroll=True)
-    def _(own):
+    fields = []
+    for own in range(OWN):
         rows = pl.ds(own, LINES, stride=OWN)
         cells = recv1[rows, :]
-        flags = jnp.broadcast_to(cells[:, MASK_LANE : MASK_LANE + 1], (LINES, LANES))
-        wall[own] = jnp.where(lane == 0, 1.0, 1.0 - flags)
         here, differences = beside_terms(cells, beside[1, rows, :], beside[0, rows, :] * inside)
-        pair[own] = to_spectrum(own, jnp.concatenate([here, differences * upward], axis=1))
+        fields.append(jnp.concatenate([here, differences * upward], axis=1))
+    for own, field in enumerate(fields):
+        pair[own] = to_spectrum(own, field)
 
     advance(pair, 0)
     advance(pair, LANES)
@@ -409,9 +413,8 @@
 
     advance(spectrum, 0)
 
-    @pl.loop(0, OWN, unroll=True)
-    def _(own):
-        send2[pl.ds(own, LINES, stride=OWN), :] = from_spectrum(own, spectrum[own])
+    for own, lines in enumerate([from_spectrum(own, spectrum[own]) for own in range(OWN)]):
+        send2[pl.ds(own, LINES, stride=OWN), :] = lines
 
     my_tile = pl.ds(pl.multiple_of((my_line + 1) * OWN, OWN), OWN)
 

time: 54.3 us -> 54.2 us (level)
  no operation moved by 1% of the time
where the time goes in v4:
time: 54.2 us; the launch traced here: 53.9 us
  Pallas kernels  53.2 us (98%)
  local copies, waits for them, and re-layouts  0.78 us (1%)
    pallas_call x1, Pallas kernels, local(): pl.pallas_call(kernel, out_shape=pltpu.VMEM((MOMENTS * OWN, LINES), F32),...  53.2 us

profile of v4, /device:TPU:1, one launch (start us, length us, event | category | flops | bytes accessed | tf_op | source)
XLA Modules:
  0.0 53.9 jit_solution(3684102786893818941)
XLA Ops:
  0.0 53.2 %duct.1 = f32[960,128]{1,0:T(8,128)S(1)} custom-call(f32[960,128]{1,0:T(8,128)} %bitcast.4, s32[8,128]{1,0:T(8,128)} %mask_h.1, f32[120,120]{1,0:T(8,128)} %c_h.1, f32[1,120]{1,0:T(1,128)} %bitcast.5, bf16[128,384]{1,0:T(8,128)(2,1)} %constant.14.clone.to_modes_h, bf16[8,288,128]{2,1,0:T(8,128)(2,1)} %constant.15.clone.forward_h, ...), custom_call_target="tpu_custom_call" | custom-call | tf_op jit(solution)/shard_map/duct/pallas_call | solution.py:495
  53.2 0.8 %copy.13 = f32[120,8,128]{2,1,0:T(8,128)} copy(f32[120,8,128]{2,1,0:T(8,128)S(1)} %bitcast.3) | data formatting | bytes 983040

commit v5 on v4

--- a/solution.py
+++ b/solution.py
@@ -345,7 +345,7 @@
     def advance(spectrum, start):
         lanes = pl.ds(start, LANES)
 
-        @pl.loop(0, BLOCKS, unroll=3)
+        @pl.loop(0, BLOCKS, unroll=True)
         def _(block):
             at = pl.multiple_of(block * 8, 8)
             re, im = pl.ds(at, 8), pl.ds(pl.multiple_of(HALF + at, 8), 8)
@@ -430,6 +430,10 @@
             device_id_type=MESH,
         ).start()
 
+    for own in range(OWN):
+        flags = send1[pl.ds(own, LINES, stride=OWN), :][:, MASK_LANE : MASK_LANE + 1]
+        wall[own] = jnp.where(lane == 0, 1.0, 1.0 - jnp.broadcast_to(flags, (LINES, LANES)))
+
     recv2[my_tile, :] = send2[pl.ds(pl.multiple_of(me * OWN, OWN), OWN), :]
     outside = pl.ds(pl.multiple_of(slab * (LINES + 1) * OWN, OWN), OWN)
     recv2[outside, :] = jnp.zeros((OWN, LANES), F32)
@@ -464,15 +468,11 @@
 
     beyond.wait()
 
-    def keep_here(own):
-        flags = send1[pl.ds(own, LINES, stride=OWN), :][:, MASK_LANE : MASK_LANE + 1]
-        return jnp.where(lane == 0, 1.0, 1.0 - jnp.broadcast_to(flags, (LINES, LANES)))
-
     fields = []
     for own in range(OWN):
         before, here, after = (recv2[pl.ds(tile * OWN + own, LINES, stride=OWN), :] for tile in range(3))
         fields.append(beside_terms(here, after, before))
-    for own, f in enumerate(finish(fields, [functools.partial(keep_here, own) for own in range(OWN)], collide)):
+    for own, f in enumerate(finish(fields, [functools.partial(wall.__getitem__, own) for own in range(OWN)], collide)):
         out_ref[pl.ds(own, MOMENTS, stride=OWN), :] = f.T[:MOMENTS]
 
     @pl.loop(0, OWN)

time: 54.2 us -> 53.7 us (level)
  no operation moved by 1% of the time
where the time goes in v5:
time: 53.7 us; the launch traced here: 53.5 us
  Pallas kernels  52.7 us (98%)
  local copies, waits for them, and re-layouts  0.78 us (1%)
    pallas_call x1, Pallas kernels, local(): pl.pallas_call(kernel, out_shape=pltpu.VMEM((MOMENTS * OWN, LINES), F32),...  52.7 us

profile of v5, /device:TPU:1, one launch (start us, length us, event | category | flops | bytes accessed | tf_op | source)
XLA Modules:
  0.0 53.5 jit_solution(13847700342109784808)
XLA Ops:
  0.0 52.7 %duct.1 = f32[960,128]{1,0:T(8,128)S(1)} custom-call(f32[960,128]{1,0:T(8,128)} %bitcast.4, s32[8,128]{1,0:T(8,128)} %mask_h.1, f32[120,120]{1,0:T(8,128)} %c_h.1, f32[1,120]{1,0:T(1,128)} %bitcast.5, bf16[128,384]{1,0:T(8,128)(2,1)} %constant.14.clone.to_modes_h, bf16[8,288,128]{2,1,0:T(8,128)(2,1)} %constant.15.clone.forward_h, ...), custom_call_target="tpu_custom_call" | custom-call | tf_op jit(solution)/shard_map/duct/pallas_call | solution.py:495
  52.7 0.8 %copy.13 = f32[120,8,128]{2,1,0:T(8,128)} copy(f32[120,8,128]{2,1,0:T(8,128)S(1)} %bitcast.3) | data formatting | bytes 983040
